TPU v7x, 256 devices: a whole 4x4x8 slice. The times are simulated.
256 devices in a mesh: fsdp: 4 (over x_lo, core), dp: 64 (over x_hi, y, z).
Axes of the slice: x: 4 (x_hi: 2, x_lo: 2; x = x_hi * 2 + x_lo), y: 4, z: 8, core: 2. Of those that a mesh axis runs over, the one named last changes fastest.
Arguments:
- inputs: bfloat16 [32768, 2048], P('dp', 'fsdp'), may hold values from -16 to 16
- cotangent: bfloat16 [32768, 7168], P('dp', 'fsdp'), may hold values from -6 to 6
- weight: bfloat16 [2048, 7168], P(None, 'fsdp'), may hold values from -0.125 to 0.125
- master: float32 [2048, 7168], P('dp', 'fsdp'), may hold values from -0.125 to 0.125
- first_moment: float32 [2048, 7168], P('dp', 'fsdp'), may hold values from -6 to 6
- second_moment: float32 [2048, 7168], P('dp', 'fsdp'), may hold values from 0.1 to 0.4
Outputs:
- input_grad: bfloat16 [32768, 2048], P('dp', 'fsdp')
- new_master: float32 [2048, 7168], P('dp', 'fsdp')
- new_first: float32 [2048, 7168], P('dp', 'fsdp')
- new_second: float32 [2048, 7168], P('dp', 'fsdp')
All inputs are finite; a program needn't handle non-finite values.
Results may differ from a plain program's by a relative error of at most 0.00055.
Values may be sent and summed in bfloat16 or wider, within the bound.
A program may use at most 128 MiB of HBM per device.

v0:
```python
import jax
import jax.numpy as jnp
from jax import lax
from jax.sharding import PartitionSpec as P


def adamw_update(grad, master, first_moment, second_moment):
    new_first = 0.9 * first_moment + 0.1 * grad
    new_second = 0.95 * second_moment + 0.05 * grad * grad
    corrected = new_first / (1.0 - 0.9**10) / (jnp.sqrt(new_second / (1.0 - 0.95**10)) + 1e-08)
    new_master = master - 0.001 * (corrected + 0.1 * master)
    return (new_master, new_first, new_second)


def local(inputs, cotangent, weight, master, first_moment, second_moment):
    token_count = inputs.shape[0]
    norm_factor = float(lax.axis_size("dp") * token_count) ** (-0.5)
    local_grad = lax.dot_general(
        lax.all_gather(inputs, "fsdp", axis=1, tiled=True),
        cotangent,
        (((0,), (0,)), ((), ())),
        preferred_element_type=jnp.float32,
    )
    summed = lax.psum_scatter(local_grad, "dp", scatter_dimension=0, tiled=True)
    partial_sum = lax.psum_scatter(
        lax.dot_general(
            weight, cotangent, (((1,), (1,)), ((), ())), preferred_element_type=jnp.float32
        ),
        "fsdp",
        scatter_dimension=0,
        tiled=True,
    )
    input_grad = partial_sum.T.astype(jnp.bfloat16)
    grad = summed * norm_factor
    new_master, new_first, new_second = adamw_update(grad, master, first_moment, second_moment)
    return (input_grad, new_master, new_first, new_second)


def solution(mesh):
    in_specs = (
        P("dp", "fsdp"),
        P("dp", "fsdp"),
        P(None, "fsdp"),
        P("dp", "fsdp"),
        P("dp", "fsdp"),
        P("dp", "fsdp"),
    )
    out_specs = (P("dp", "fsdp"), P("dp", "fsdp"), P("dp", "fsdp"), P("dp", "fsdp"))
    return jax.shard_map(local, mesh=mesh, in_specs=in_specs, out_specs=out_specs, check_vma=False)
```

profile of v0, /device:TPU:2, one launch (start us, length us, event | category | flops | bytes accessed | tf_op | source)
XLA Modules:
  0.0 503.7 jit_solution(3406423064837121347)
XLA Ops:
  7.2 0.0 copy-start
  7.2 0.0 all-gather.2.cloned.1.call-start
  7.2 0.7 all-gather.2.cloned.1.call-update
  7.9 0.0 reduce-scatter.3.cloned.1.call-start
  8.0 0.7 copy-done
  8.7 8.8 %fusion = f32[2048,512]{1,0:T(8,128)} fusion(bf16[2048,1792]{1,0:T(8,128)(2,1)} %param.8, bf16[512,1792]{1,0:T(8,128)(2,1)S(1)} %copy-done), kind=kOutput, calls=%fused_computation.4 | convolution fusion | flops 3758096384 | bytes 13369344 | tf_op jit(solution)/shard_map/dot_general | solution.py:26
  17.4 0.0 reduce-scatter.3.cloned.1.call-update
  17.5 0.0 reduce-scatter.5.cloned.1.call-start
  17.5 25.2 %all-gather.2.cloned.1.call-done = bf16[512,2048]{1,0:T(8,128)(2,1)} async-done(((bf16[512,512]{1,0:T(8,128)(2,1)}), bf16[512,2048]{1,0:T(8,128)(2,1)}) %all-gather.2.cloned.1.call-update) | async-done | bytes 2097168 | tf_op jit(solution)/shard_map/all_gather | solution.py:19
  42.8 9.3 %fusion.1 = f32[2048,1792]{1,0:T(8,128)} fusion(bf16[512,2048]{1,0:T(8,128)(2,1)} %all-gather.2.cloned.1.call-done, bf16[512,1792]{1,0:T(8,128)(2,1)S(1)} %copy-done), kind=kOutput, calls=%fused_computation.5 | convolution fusion | flops 3758096384 | bytes 18612224 | tf_op jit(solution)/shard_map/dot_general | solution.py:18
  52.1 0.0 reduce-scatter.5.cloned.1.call-update
  52.1 0.0 copy-start.1
  52.1 0.0 copy-start.2
  52.1 0.0 copy-start.3
  52.1 42.0 %reduce-scatter.3.cloned.1.call-done = f32[512,512]{1,0:T(8,128)} async-done(((f32[2048,512]{1,0:T(8,128)}), f32[512,512]{1,0:T(8,128)}) %reduce-scatter.3.cloned.1.call-update) | async-done | bytes 1048592 | tf_op jit(solution)/shard_map/reduce_scatter | solution.py:25
  94.2 1.3 convert_bitcast_fusion
  95.4 1.0 copy.10
  96.4 398.8 %reduce-scatter.5.cloned.1.call-done = f32[32,1792]{1,0:T(8,128)} async-done(((f32[2048,1792]{1,0:T(8,128)}), f32[32,1792]{1,0:T(8,128)}) %reduce-scatter.5.cloned.1.call-update) | async-done | bytes 229392 | tf_op jit(solution)/shard_map/reduce_scatter | solution.py:24
  495.3 0.0 copy-done.1
  495.3 0.0 copy-done.2
  495.3 0.0 copy-done.3
  495.3 1.9 multiply_subtract_fusion
Async XLA Ops:
  7.2 1.5 copy-start
  7.2 35.6 %all-gather.2.cloned.1.call-start = ((), (), s32[]{:S(2)}) async-start(), calls=%async_computation.3 | async-start | bytes 2621440 | tf_op jit(solution)/shard_map/all_gather | solution.py:19
  7.9 86.2 %reduce-scatter.3.cloned.1.call-start = ((), (), s32[]{:S(2)}) async-start(), calls=%async_computation.2 | async-start | bytes 5242880 | tf_op jit(solution)/shard_map/reduce_scatter | solution.py:25
  17.5 477.8 %reduce-scatter.5.cloned.1.call-start = ((), (), s32[]{:S(2)}) async-start(), calls=%async_computation.4 | async-start | bytes 14909440 | tf_op jit(solution)/shard_map/reduce_scatter | solution.py:24
  52.1 443.2 %copy-start.1 = (f32[32,1792]{1,0:T(8,128)S(1)}, f32[32,1792]{1,0:T(8,128)}, u32[]{:S(2)}) copy-start(f32[32,1792]{1,0:T(8,128)} %param.9) | copy-start | bytes 688132
  52.1 443.2 %copy-start.2 = (f32[32,1792]{1,0:T(8,128)S(1)}, f32[32,1792]{1,0:T(8,128)}, u32[]{:S(2)}) copy-start(f32[32,1792]{1,0:T(8,128)} %param.10) | copy-start | bytes 688132
  52.1 443.2 %copy-start.3 = (f32[32,1792]{1,0:T(8,128)S(1)}, f32[32,1792]{1,0:T(8,128)}, u32[]{:S(2)}) copy-start(f32[32,1792]{1,0:T(8,128)} %param.11) | copy-start | bytes 688132
Sparse Core Ops, SparseCore 0:
  9.8 32.8 all-gather.1
  45.3 48.8 reduce-scatter.2
  96.9 398.3 reduce-scatter.4
where the time goes:
time: 504 us
  waiting for transfers between devices  467 us (93%)
  matrix products  18.1 us (4%)
  between operations  13.8 us (3%)
    reduce_scatter x1, waiting for transfers between devices, local(): summed = lax.psum_scatter(local_grad, 'dp', scatter_dimension=0, tiled=True)  399 us
    reduce_scatter x1, waiting for transfers between devices, local(): lax.psum_scatter(lax.dot_general(weight, cotangent, (((1,), (1,)), ((), (...  42 us
    all_gather x1, waiting for transfers between devices, local(): lax.all_gather(inputs, 'fsdp', axis=1, tiled=True)  25.2 us
  transfers between devices with their start and end apart: 3, of which 3 were waited for; matrix products, arithmetic and copies ran while one was open for 4% of the time, Pallas kernels for 0%

commit v1 on v0

v1 whole, which is shorter than its diff:
```python
import jax
import jax.numpy as jnp
from jax import lax
from jax.experimental import pallas as pl
from jax.experimental.pallas import tpu as pltpu
from jax.sharding import PartitionSpec as P

MESH = pl.DeviceIdType.MESH
F32, BF16 = jnp.float32, jnp.bfloat16
TOK, FEAT, COLS = 512, 512, 1792
LIFT = 1024.0
STREAMS = (
    (("a", 384), ("a", 256), ("a", 384), ("h", 768)),
    (("a", 512), ("a", 512), ("b", 256), ("b", 512)),
)
ORDER = (
    ("sendx",), ("ig0",), ("mg", 0, 3, 0), ("mg", 0, 2, 1), ("hz0", 0, 3, "o", 1), ("hz0", 0, 3, "m", 0),
    ("mg", 0, 2, 0), ("ay", 0, 2, "o", 1), ("mg", 0, 1, 1), ("mg", 0, 3, 1), ("mg", 0, 1, 0),
    ("ay", 0, 1, "m", 0), ("mg", 0, 0, 0), ("hz1", 0, 3, "m", 0), ("ay", 0, 2, "m", 0),
    ("hz1", 0, 3, "o", 1), ("ay", 0, 1, "o", 1), ("ig1",), ("iadd",), ("hz0", 0, 3, "o", 2),
    ("mg", 0, 0, 1), ("ay", 0, 0, "m", 0), ("hz0", 0, 3, "m", 1), ("ay", 0, 0, "o", 1),
    ("hz1", 0, 3, "o", 2), ("ay", 0, 1, "m", 1), ("hz1", 0, 3, "m", 1), ("ig2",), ("hz0", 0, 3, "o", 3),
    ("ig3",), ("ay", 0, 2, "m", 1), ("fwd",), ("mg", 1, 3, 0), ("mg", 1, 2, 0), ("mg", 1, 0, 0),
    ("hz1", 0, 3, "o", 3), ("hz0", 0, 3, "m", 2), ("mg", 1, 1, 0), ("mg", 1, 3, 1), ("bz", 1, 3, "o", 1),
    ("mg", 1, 1, 1), ("ay", 0, 0, "m", 1), ("mg", 1, 2, 1), ("bz", 1, 3, "m", 0), ("ay", 1, 1, "o", 1),
    ("bz", 1, 2, "m", 0), ("ay", 1, 1, "m", 0), ("mg", 1, 0, 1), ("ay", 1, 0, "m", 0), ("bz", 1, 2, "o", 1),
    ("ay", 0, 2, "f"), ("az", 0, 2, "m", 0), ("ay", 0, 1, "f"), ("xo", 0, 1), ("hz0", 0, 3, "m", 3),
    ("ay", 1, 0, "o", 1), ("hz1", 0, 3, "m", 2), ("bz", 1, 3, "o", 2), ("az", 0, 2, "o", 1),
    ("az", 0, 1, "o", 1), ("az", 0, 1, "m", 0), ("xo", 0, 2), ("bz", 1, 3, "m", 1), ("ay", 0, 0, "f"),
    ("az", 0, 0, "m", 0), ("bz", 1, 2, "m", 1), ("bz", 1, 2, "o", 2), ("az", 0, 2, "m", 1), ("xo", 0, 0),
    ("az", 0, 0, "o", 1), ("hz0", 0, 3, "f"), ("bz", 1, 3, "o", 3), ("az", 0, 2, "o", 2),
    ("az", 0, 1, "o", 2), ("hz1", 0, 3, "m", 3), ("az", 0, 1, "m", 1), ("ay", 1, 1, "m", 1),
    ("bz", 1, 2, "o", 3), ("az", 0, 0, "o", 2), ("bz", 1, 3, "m", 2), ("az", 0, 0, "m", 1),
    ("az", 0, 2, "o", 3), ("ay", 1, 0, "m", 1), ("bz", 1, 2, "m", 2), ("az", 0, 1, "o", 3),
    ("az", 0, 2, "m", 2), ("ifin",), ("az", 0, 0, "o", 3), ("hz1", 0, 3, "f"), ("az", 0, 1, "m", 2),
    ("by", 0, 3, "m", 0), ("ay", 1, 1, "f"), ("az", 1, 1, "o", 1), ("az", 1, 1, "m", 0),
    ("by", 0, 3, "o", 1), ("xo", 1, 1), ("xo", 0, 3), ("bz", 1, 3, "m", 3), ("az", 0, 0, "m", 2),
    ("ay", 1, 0, "f"), ("az", 1, 0, "m", 0), ("bz", 1, 2, "m", 3), ("by", 0, 3, "m", 1),
    ("az", 0, 2, "m", 3), ("az", 1, 1, "o", 2), ("az", 0, 1, "m", 3), ("az", 1, 1, "m", 1),
    ("az", 1, 0, "o", 1), ("xo", 1, 0), ("bz", 1, 3, "f"), ("by", 1, 3, "m", 0), ("az", 0, 0, "m", 3),
    ("xo", 1, 3), ("by", 1, 3, "o", 1), ("az", 1, 0, "m", 1), ("az", 1, 1, "o", 3), ("by", 0, 3, "f"),
    ("az", 1, 0, "o", 2), ("bz", 1, 2, "f"), ("by", 1, 2, "m", 0), ("xo", 1, 2), ("by", 1, 2, "o", 1),
    ("az", 1, 1, "m", 2), ("by", 1, 3, "m", 1), ("az", 0, 2, "f"), ("az", 1, 0, "m", 2), ("az", 0, 1, "f"),
    ("az", 0, 0, "f"), ("az", 1, 0, "o", 3), ("by", 1, 2, "m", 1), ("az", 1, 1, "m", 3),
    ("az", 1, 0, "m", 3), ("by", 1, 3, "f"), ("by", 1, 2, "f"), ("az", 1, 1, "f"), ("az", 1, 0, "f"),
)


def encode(x):
    s = x * x
    return (s * (x * jnp.abs(x))).astype(BF16)


def decode(c):
    c = c.astype(F32)
    t = lax.rsqrt(lax.rsqrt(jnp.abs(c)))
    return jnp.where(c < 0, -t, t)


def adamw_update(grad, master, first_moment, second_moment):
    new_first = 0.9 * first_moment + 0.1 * grad
    new_second = 0.95 * second_moment + 0.05 * grad * grad
    corrected = new_first / (1.0 - 0.9**10) / (jnp.sqrt(new_second / (1.0 - 0.95**10)) + 1e-08)
    new_master = master - 0.001 * (corrected + 0.1 * master)
    return (new_master, new_first, new_second)


STAGES = {"a": ("ay", "az"), "b": ("bz", "by"), "h": ("hz0", "hz1", "by")}
RING = {"ay": (4, 8), "az": (8, 1), "bz": (8, 4), "hz0": (8, 2), "hz1": (8, 2), "by": (4, 1)}
LAST = ("az", "by")


def streams():
    for ph, cut in enumerate(STREAMS):
        first = 0
        for s, (kind, width) in enumerate(cut):
            yield ph, s, kind, first, width
            first += width


def kernel(norm, x_hbm, c_hbm, w_hbm, grad_out, ig_out, *scratch):
    x_in, xt, cot, w, g, pc_s, pc_r, pp_s, pp_r = scratch[:9]
    ld_sem, xt_ss, xt_rs, pc_ss, pc_rs, pp_ss, pp_rs = scratch[9:16]
    rest = list(scratch[16:])
    buffers = {}
    spans = {}
    for ph, s, kind, first, width in streams():
        spans[ph, s] = pl.ds(first, width), width
        for stage in STAGES[kind]:
            buffers[stage, ph, s], rest = rest[:4], rest[4:]

    f, d = lax.axis_index("fsdp"), lax.axis_index("dp")
    x_lo, core = f // 2, f % 2
    x_hi, y, z = d // 32, (d // 8) % 4, d % 8
    turn = 1 - 2 * core
    mine = (x_lo + x_hi) % 2
    other_core = {"dp": d, "fsdp": x_lo * 2 + (1 - core)}
    x_lo_peer = {"dp": d, "fsdp": (1 - x_lo) * 2 + core}
    x_hi_peer = {"dp": (1 - x_hi) * 32 + y * 8 + z, "fsdp": f}

    def y_peer(step, across=0):
        return {"dp": (x_hi + across) % 2 * 32 + ((y + 4 + step) % 4) * 8 + z, "fsdp": f}

    def z_peer(step, across=0):
        return {"dp": (x_hi + across) % 2 * 32 + y * 8 + (z + 8 + step) % 8, "fsdp": f}

    barrier = pltpu.get_barrier_semaphore()
    partners = [other_core, x_lo_peer, x_hi_peer]
    partners += [peer(step, side) for peer in (y_peer, z_peer) for step in (1, -1) for side in (0, 1)]
    for p in partners:
        pl.semaphore_signal(barrier, inc=1, device_id=p, device_id_type=MESH)
    load_x = pltpu.make_async_copy(x_hbm, x_in, ld_sem.at[0])
    load_x.start()
    load_c = pltpu.make_async_copy(c_hbm, cot, ld_sem.at[1])
    load_c.start()
    blocks = ((1 - x_lo) * 2 + (1 - core), (1 - x_lo) * 2 + core, x_lo * 2 + (1 - core), f)
    load_w = []
    for i, b in enumerate(blocks):
        copy = pltpu.make_async_copy(w_hbm.at[pl.ds(b * FEAT, FEAT)], w.at[i], ld_sem.at[2 + i])
        copy.start()
        load_w.append(copy)

    sends = []

    def copy_to(src, dst, ss, rs, peer):
        return pltpu.make_async_remote_copy(
            src_ref=src, dst_ref=dst, send_sem=ss, recv_sem=rs, device_id=peer, device_id_type=MESH
        )

    def send(*args):
        copy = copy_to(*args)
        copy.start()
        sends.append(copy)
        return copy

    def pieces(n, body):
        if n == 1:
            body(0)
        else:
            pl.loop(0, n)(body)

    def grad_block(ph, s, block):
        span, width = spans[ph, s]
        half = core if block == 0 else 1 - core
        tile = 256 if width % 256 == 0 else width

        def body(j):
            cols = pl.ds(pl.multiple_of(span.start + j * tile, 128), tile)
            part = jnp.dot(xt[2 * ph + block], cot[:, cols], preferred_element_type=F32)
            g[ph, pl.ds(half * 2, 2), :, :, cols] = part.reshape(2, 8, 32, tile)

        pieces(width // tile, body)

    def input_block(i, write):
        load_w[i].wait()

        @pl.loop(0, 2)
        def _(j):
            rows = pl.ds(pl.multiple_of(j * 256, 256), 256)
            part = lax.dot_general(
                cot[...], w[i, rows, :], (((1,), (1,)), ((), ())), preferred_element_type=F32
            )
            write(rows, part)

    def rows_loop(body):
        @pl.loop(0, 16)
        def _(i):
            body(pl.ds(pl.multiple_of(i * 32, 32), 32))

    def view(stage, ph, s, to, i):
        cols = spans[ph, s][0]
        if stage == "ay":
            return ph, to, i, slice(None), cols
        if stage == "az":
            return ph, y, to, slice(None), cols
        if stage == "bz":
            return ph, i, to, slice(None), cols
        if stage[:2] == "hz":
            half = core if stage == "hz0" else 1 - core
            return ph, 2 * half + i, to, slice(None), cols
        return ph, to, z, slice(None), cols

    def ring(stage):
        n, count = RING[stage]
        return (n, count, y, y_peer) if stage[1] == "y" else (n, count, z, z_peer)

    def slot_of(n, way, k):
        return k if way > 0 else n // 2 + k - 1

    def came(stage, ph, s, way, k):
        n, _, _, peer = ring(stage)
        s_buf, r_buf, ss, rs = buffers[stage, ph, s]
        m = slot_of(n, way, k)
        copy_to(s_buf.at[m], r_buf.at[m], ss.at[m], rs.at[m], peer(way * turn)).wait_recv()
        return r_buf.at[m]

    def hop(stage, ph, s, way, k):
        n, count, place, peer = ring(stage)
        s_buf, r_buf, ss, rs = buffers[stage, ph, s]
        to = (place + n + way * turn * (n // 2 - k)) % n
        m = slot_of(n, way, k)
        first = k == (0 if way > 0 else 1)
        got = None if first else came(stage, ph, s, way, k - 1)

        def body(i):
            part = g[view(stage, ph, s, to, i)]
            if not first:
                part = part + decode(got[i])
            s_buf[m, i] = encode(part)

        pieces(count, body)
        if stage in LAST and k == n // 2 - 1:
            away = (mine + ph) % 2
            to_slot = m + away * ((n - 1 if way > 0 else n) - m)
            send(s_buf.at[m], r_buf.at[to_slot], ss.at[m], rs.at[to_slot], peer(way * turn, away))
        else:
            send(s_buf.at[m], r_buf.at[m], ss.at[m], rs.at[m], peer(way * turn))

    def finish(stage, ph, s):
        n, count, place, _ = ring(stage)
        last = [came(stage, ph, s, way, n // 2 - 1) for way in (1, -1)]

        def body(i):
            own = view(stage, ph, s, place, i)
            g[own] = g[own] + decode(last[0][i]) + decode(last[1][i])

        pieces(count, body)

    def own_part(stage, ph, s):
        n, _, place, _ = ring(stage)
        s_buf, r_buf, ss, rs = buffers[stage, ph, s]
        copy = copy_to(s_buf.at[n - 1], r_buf.at[n + 1], ss.at[n - 1], rs.at[n + 1], x_hi_peer)
        return view(stage, ph, s, place, 0), s_buf, copy

    def own_across(stage, ph, s):
        @pl.when(mine != ph)
        def _():
            own, s_buf, copy = own_part(stage, ph, s)
            s_buf[RING[stage][0] - 1, 0] = encode(g[own])
            copy.start()

    def last_finish(stage, ph, s):
        n, _, place, _ = ring(stage)
        s_buf, r_buf, ss, rs = buffers[stage, ph, s]

        @pl.when(mine == ph)
        def _():
            total = g[view(stage, ph, s, place, 0)]
            slots = (slot_of(n, 1, n // 2 - 1), slot_of(n, -1, n // 2 - 1), n - 1, n, n + 1)
            for m in slots:
                copy_to(s_buf.at[0], r_buf.at[m], ss.at[0], rs.at[m], x_hi_peer).wait_recv()
                total = total + decode(r_buf[m, 0])
            grad_out[:, spans[ph, s][0]] = total * norm

    def to_buffer(buf, k):
        def write(rows, part):
            buf[k, :, rows] = part

        return write

    flight = {}

    def send_features():
        flight["core"] = send(xt.at[0], xt.at[1], xt_ss.at[0], xt_rs.at[0], other_core)
        flight["chip"] = send(xt.at[0], xt.at[2], xt_ss.at[1], xt_rs.at[1], x_lo_peer)
        load_c.wait()

    def pass_features():
        flight["chip"].wait_recv()
        flight["pass"] = send(xt.at[2], xt.at[3], xt_ss.at[2], xt_rs.at[2], other_core)

    def partial_input_grad(i):
        input_block(i, to_buffer(pc_s if i % 2 == 0 else pp_s, i // 2))
        if i % 2 == 0:
            k = i // 2
            flight["pc", k] = send(pc_s.at[k], pc_r.at[k], pc_ss.at[k], pc_rs.at[k], other_core)

    def chip_sum():
        flight["pc", 0].wait_recv()

        def body(rows):
            pp_s[0, rows, :] = pp_s[0, rows, :] + pc_r[0, rows, :]

        rows_loop(body)
        flight["pp"] = send(pp_s.at[0], pp_r.at[0], pp_ss.at[0], pp_rs.at[0], x_lo_peer)

    def input_grad_sum():
        flight["pc", 1].wait_recv()
        flight["pp"].wait_recv()

        def body(rows):
            total = pp_s[1, rows, :] + pc_r[1, rows, :] + pp_r[0, rows, :]
            ig_out[rows, :] = total.astype(BF16)

        rows_loop(body)

    load_x.wait()
    xt[0] = (x_in[...] * jnp.array(LIFT, BF16)).T
    pl.semaphore_wait(barrier, len(partners))

    waits = {(0, 1): "core", (1, 1): "pass"}
    waited = set()
    for what, *at in ORDER:
        if what == "sendx":
            send_features()
        elif what == "fwd":
            pass_features()
        elif what[:2] == "ig":
            partial_input_grad(int(what[2]))
        elif what == "iadd":
            chip_sum()
        elif what == "ifin":
            input_grad_sum()
        elif what == "mg":
            ph, s, block = at
            key = waits.get((ph, block))
            if key and key not in waited:
                flight[key].wait_recv()
                waited.add(key)
            grad_block(ph, s, block)
        elif what == "xo":
            own_across(STAGES[STREAMS[at[0]][at[1]][0]][-1], *at)
        elif at[2] == "f":
            (last_finish if what in LAST else finish)(what, *at[:2])
        else:
            hop(what, at[0], at[1], 1 if at[2] == "m" else -1, at[3])
    for copy in sends:
        copy.wait_send()
    for ph, s, kind, *_ in streams():

        @pl.when(mine != ph)
        def _():
            own_part(STAGES[kind][-1], ph, s)[2].wait_send()


def reduce_all(norm, inputs, cotangent, weight):
    dma = pltpu.SemaphoreType.DMA
    nm = lambda *s: pltpu.VMEM(s, BF16)
    rings = []
    for _, _, kind, _, width in streams():
        for stage in STAGES[kind]:
            n, count = RING[stage]
            sent, came = (n, n + 2) if stage in LAST else (n - 1, n - 1)
            rings += [nm(sent, count, 32, width), nm(came, count, 32, width), dma((sent,)), dma((came,))]
    any_ = pl.BlockSpec(memory_space=pl.ANY)
    vm = pl.BlockSpec(memory_space=pltpu.VMEM)
    return pl.pallas_call(
        lambda *refs: kernel(norm, *refs),
        out_shape=(
            jax.ShapeDtypeStruct((32, COLS), F32),
            jax.ShapeDtypeStruct((TOK, FEAT), BF16),
        ),
        in_specs=[any_, any_, any_],
        out_specs=(vm, vm),
        scratch_shapes=[
            nm(TOK, FEAT), nm(4, FEAT, TOK), nm(TOK, COLS), nm(4, FEAT, COLS),
            pltpu.VMEM((2, 4, 8, 32, COLS), F32),
            pltpu.VMEM((2, TOK, FEAT), F32), pltpu.VMEM((2, TOK, FEAT), F32),
            pltpu.VMEM((2, TOK, FEAT), F32), pltpu.VMEM((1, TOK, FEAT), F32),
            dma((6,)), dma((3,)), dma((3,)),
            dma((2,)), dma((2,)), dma((1,)), dma((1,)),
            *rings,
        ],
        compiler_params=pltpu.CompilerParams(
            collective_id=1, has_side_effects=True, vmem_limit_bytes=60 * 2**20
        ),
        cost_estimate=pl.CostEstimate(flops=7516192768, bytes_accessed=12000000, transcendentals=0),
        name="reduce_all",
    )(inputs, cotangent, weight)


def update_kernel(grad, master, first, second, ig, new_master, new_first, new_second, ig_out):
    ig_out[...] = ig[...]
    out = adamw_update(grad[...], master[...], first[...], second[...])
    new_master[...], new_first[...], new_second[...] = out


def update(grad, master, first, second, input_grad):
    rows, tall = pl.BlockSpec((16, COLS), lambda i: (i, 0)), pl.BlockSpec((256, FEAT), lambda i: (i, 0))
    like = lambda a: jax.ShapeDtypeStruct(a.shape, a.dtype)
    return pl.pallas_call(
        update_kernel,
        out_shape=(like(master), like(first), like(second), like(input_grad)),
        grid=(2,),
        in_specs=[rows, rows, rows, rows, tall],
        out_specs=(rows, rows, rows, tall),
        name="update",
    )(grad, master, first, second, input_grad)


def local(inputs, cotangent, weight, master, first_moment, second_moment):
    token_count = inputs.shape[0]
    norm = float(lax.axis_size("dp") * token_count) ** (-0.5) / LIFT
    grad, input_grad = reduce_all(norm, inputs, cotangent, weight)
    out = update(grad, master, first_moment, second_moment, input_grad)
    new_master, new_first, new_second, input_grad = out
    return (input_grad, new_master, new_first, new_second)


def solution(mesh):
    split = P("dp", "fsdp")
    in_specs = (split, split, P(None, "fsdp"), split, split, split)
    return jax.shard_map(
        local, mesh=mesh, in_specs=in_specs, out_specs=(split,) * 4, check_vma=False
    )
```

time: 504 us -> 70.5 us (0.14)
  waiting for transfers between devices: 467 us -> 0 us
  Pallas kernels: 0 us -> 69.7 us
  matrix products: 18.1 us -> 0 us
  between operations: 13.8 us -> 0.64 us
    reduce_scatter x2 -> x0, waiting for transfers between devices: 441 us -> none  [the longest x1 399 us: local(): summed = lax.psum_scatter(local_grad, 'dp', scatter_dimension=0, tiled=True)]
    pallas_call x0 -> x2, Pallas kernels: none -> 69.7 us  [the longest x1 67.5 us: reduce_all(): pl.pallas_call(lambda *refs: kernel(norm, *refs), out_shape=(jax.ShapeDty...]
    all_gather x1 -> x0, waiting for transfers between devices: 25.2 us -> none  [local(): lax.all_gather(inputs, 'fsdp', axis=1, tiled=True)]
    dot_general x2 -> x0, matrix products: 18.1 us -> none  [the longest x1 9.34 us: local(): lax.dot_general(lax.all_gather(inputs, 'fsdp', axis=1, tiled=True), cotan...]
  transfers between devices with their start and end apart: 3 -> 0, of which waited for: 3 -> 0; matrix products, arithmetic and copies ran while one was open for 4% -> 0% of each run, Pallas kernels for 0% -> 0%
where the time goes in v1:
time: 70.5 us; the launch traced here: 70.4 us
  Pallas kernels  69.7 us (99%)
    pallas_call x1, Pallas kernels, reduce_all(): pl.pallas_call(lambda *refs: kernel(norm, *refs), out_shape=(jax.ShapeDty...  67.5 us
    pallas_call x1, Pallas kernels, update(): pl.pallas_call(update_kernel, out_shape=(like(master), like(first), like(...  2.29 us

profile of v1, /device:TPU:2, one launch (start us, length us, event | category | flops | bytes accessed | tf_op | source)
XLA Modules:
  0.0 70.4 jit_solution(15053221662498556246)
XLA Ops:
  0.6 67.5 %reduce_all.1 = (f32[32,1792]{1,0:T(8,128)}, bf16[512,512]{1,0:T(8,128)(2,1)}) custom-call(bf16[512,512]{1,0:T(8,128)(2,1)} %refs_0_.1, bf16[512,1792]{1,0:T(8,128)(2,1)} %refs_1_.1, bf16[2048,1792]{1,0:T(8,128)(2,1)} %refs_2_.1), custom_call_target="tpu_custom_call" | custom-call | flops 7516192768 | bytes 12000000 | tf_op jit(solution)/shard_map/reduce_all/pallas_call | solution.py:347
  68.1 2.3 %update.1 = (f32[32,1792]{1,0:T(8,128)}, f32[32,1792]{1,0:T(8,128)}, f32[32,1792]{1,0:T(8,128)}, bf16[512,512]{1,0:T(8,128)(2,1)}) custom-call(f32[32,1792]{1,0:T(8,128)} %get-tuple-element.10.grad, f32[32,1792]{1,0:T(8,128)} %master.1, f32[32,1792]{1,0:T(8,128)} %first.1, f32[32,1792]{1,0:T(8,128)} %second.1, bf16[512,512]{1,0:T(8,128)(2,1)} %get-tuple-element.11.ig), custom_call_target="tpu_custom_call" | custom-call | tf_op jit(solution)/shard_map/update/pallas_call | solution.py:381

commit v2 on v1

--- a/solution.py
+++ b/solution.py
@@ -10,39 +10,36 @@
 TOK, FEAT, COLS = 512, 512, 1792
 LIFT = 1024.0
 STREAMS = (
-    (("a", 384), ("a", 256), ("a", 384), ("h", 768)),
-    (("a", 512), ("a", 512), ("b", 256), ("b", 512)),
+    (("a", 512, "r"), ("a", 384, "r"), ("h", 896, "r")),
+    (("a", 256, "t"), ("a", 512, "r"), ("a", 384, "t"), ("b", 128, "t"), ("b", 256, "t"), ("b", 256, "t")),
 )
 ORDER = (
-    ("sendx",), ("ig0",), ("mg", 0, 3, 0), ("mg", 0, 2, 1), ("hz0", 0, 3, "o", 1), ("hz0", 0, 3, "m", 0),
-    ("mg", 0, 2, 0), ("ay", 0, 2, "o", 1), ("mg", 0, 1, 1), ("mg", 0, 3, 1), ("mg", 0, 1, 0),
-    ("ay", 0, 1, "m", 0), ("mg", 0, 0, 0), ("hz1", 0, 3, "m", 0), ("ay", 0, 2, "m", 0),
-    ("hz1", 0, 3, "o", 1), ("ay", 0, 1, "o", 1), ("ig1",), ("iadd",), ("hz0", 0, 3, "o", 2),
-    ("mg", 0, 0, 1), ("ay", 0, 0, "m", 0), ("hz0", 0, 3, "m", 1), ("ay", 0, 0, "o", 1),
-    ("hz1", 0, 3, "o", 2), ("ay", 0, 1, "m", 1), ("hz1", 0, 3, "m", 1), ("ig2",), ("hz0", 0, 3, "o", 3),
-    ("ig3",), ("ay", 0, 2, "m", 1), ("fwd",), ("mg", 1, 3, 0), ("mg", 1, 2, 0), ("mg", 1, 0, 0),
-    ("hz1", 0, 3, "o", 3), ("hz0", 0, 3, "m", 2), ("mg", 1, 1, 0), ("mg", 1, 3, 1), ("bz", 1, 3, "o", 1),
-    ("mg", 1, 1, 1), ("ay", 0, 0, "m", 1), ("mg", 1, 2, 1), ("bz", 1, 3, "m", 0), ("ay", 1, 1, "o", 1),
-    ("bz", 1, 2, "m", 0), ("ay", 1, 1, "m", 0), ("mg", 1, 0, 1), ("ay", 1, 0, "m", 0), ("bz", 1, 2, "o", 1),
-    ("ay", 0, 2, "f"), ("az", 0, 2, "m", 0), ("ay", 0, 1, "f"), ("xo", 0, 1), ("hz0", 0, 3, "m", 3),
-    ("ay", 1, 0, "o", 1), ("hz1", 0, 3, "m", 2), ("bz", 1, 3, "o", 2), ("az", 0, 2, "o", 1),
-    ("az", 0, 1, "o", 1), ("az", 0, 1, "m", 0), ("xo", 0, 2), ("bz", 1, 3, "m", 1), ("ay", 0, 0, "f"),
-    ("az", 0, 0, "m", 0), ("bz", 1, 2, "m", 1), ("bz", 1, 2, "o", 2), ("az", 0, 2, "m", 1), ("xo", 0, 0),
-    ("az", 0, 0, "o", 1), ("hz0", 0, 3, "f"), ("bz", 1, 3, "o", 3), ("az", 0, 2, "o", 2),
-    ("az", 0, 1, "o", 2), ("hz1", 0, 3, "m", 3), ("az", 0, 1, "m", 1), ("ay", 1, 1, "m", 1),
-    ("bz", 1, 2, "o", 3), ("az", 0, 0, "o", 2), ("bz", 1, 3, "m", 2), ("az", 0, 0, "m", 1),
-    ("az", 0, 2, "o", 3), ("ay", 1, 0, "m", 1), ("bz", 1, 2, "m", 2), ("az", 0, 1, "o", 3),
-    ("az", 0, 2, "m", 2), ("ifin",), ("az", 0, 0, "o", 3), ("hz1", 0, 3, "f"), ("az", 0, 1, "m", 2),
-    ("by", 0, 3, "m", 0), ("ay", 1, 1, "f"), ("az", 1, 1, "o", 1), ("az", 1, 1, "m", 0),
-    ("by", 0, 3, "o", 1), ("xo", 1, 1), ("xo", 0, 3), ("bz", 1, 3, "m", 3), ("az", 0, 0, "m", 2),
-    ("ay", 1, 0, "f"), ("az", 1, 0, "m", 0), ("bz", 1, 2, "m", 3), ("by", 0, 3, "m", 1),
-    ("az", 0, 2, "m", 3), ("az", 1, 1, "o", 2), ("az", 0, 1, "m", 3), ("az", 1, 1, "m", 1),
-    ("az", 1, 0, "o", 1), ("xo", 1, 0), ("bz", 1, 3, "f"), ("by", 1, 3, "m", 0), ("az", 0, 0, "m", 3),
-    ("xo", 1, 3), ("by", 1, 3, "o", 1), ("az", 1, 0, "m", 1), ("az", 1, 1, "o", 3), ("by", 0, 3, "f"),
-    ("az", 1, 0, "o", 2), ("bz", 1, 2, "f"), ("by", 1, 2, "m", 0), ("xo", 1, 2), ("by", 1, 2, "o", 1),
-    ("az", 1, 1, "m", 2), ("by", 1, 3, "m", 1), ("az", 0, 2, "f"), ("az", 1, 0, "m", 2), ("az", 0, 1, "f"),
-    ("az", 0, 0, "f"), ("az", 1, 0, "o", 3), ("by", 1, 2, "m", 1), ("az", 1, 1, "m", 3),
-    ("az", 1, 0, "m", 3), ("by", 1, 3, "f"), ("by", 1, 2, "f"), ("az", 1, 1, "f"), ("az", 1, 0, "f"),
+    ("sendx",), ("ig0",), ("mg", 0, 1, 0), ("mg", 0, 0, 1), ("mg", 0, 1, 1), ("mg", 0, 2, 1),
+    ("hz1", 0, 2, 0), ("mg", 0, 2, 0), ("ay", 0, 1, 0), ("hz0", 0, 2, 0), ("mg", 0, 0, 0), ("ay", 0, 0, 0),
+    ("hz0", 0, 2, 4), ("hz1", 0, 2, 4), ("ay", 0, 1, 2), ("ig1",), ("iadd",), ("hz1", 0, 2, 1),
+    ("ay", 0, 0, 2), ("hz0", 0, 2, 1), ("ig2",), ("ay", 0, 1, 1), ("hz0", 0, 2, 5), ("hz1", 0, 2, 5),
+    ("ig3",), ("hz1", 0, 2, 2), ("fwd",), ("mg", 1, 0, 0), ("mg", 1, 1, 0), ("mg", 1, 2, 0),
+    ("mg", 1, 5, 0), ("mg", 1, 4, 0), ("ay", 0, 0, 1), ("mg", 1, 1, 1), ("ay", 1, 1, 0), ("ay", 1, 1, 2),
+    ("mg", 1, 4, 1), ("bz", 1, 4, 4), ("bz", 1, 4, 0), ("mg", 1, 5, 1), ("mg", 1, 2, 1), ("mg", 1, 0, 1),
+    ("ay", 1, 0, 0), ("bz", 1, 5, 0), ("ay", 1, 2, 0), ("hz0", 0, 2, 2), ("bz", 1, 5, 4), ("mg", 1, 3, 1),
+    ("ay", 1, 0, 2), ("mg", 1, 3, 0), ("bz", 1, 3, 0), ("ay", 0, 1, "f"), ("az", 0, 1, 0), ("hz0", 0, 2, 6),
+    ("ay", 1, 2, 2), ("hz1", 0, 2, 6), ("bz", 1, 4, 5), ("bz", 1, 4, 1), ("hz1", 0, 2, 3), ("bz", 1, 3, 4),
+    ("az", 0, 1, 4), ("xo", 0, 1), ("bz", 1, 5, 1), ("bz", 1, 5, 5), ("ay", 0, 0, "f"), ("az", 0, 0, 0),
+    ("az", 0, 0, 4), ("hz0", 0, 2, 3), ("xo", 0, 0), ("bz", 1, 3, 1), ("az", 0, 1, 1), ("bz", 1, 4, 2),
+    ("ay", 1, 1, 1), ("bz", 1, 4, 6), ("hz1", 0, 2, "f"), ("bz", 1, 3, 5), ("bz", 1, 5, 2), ("az", 0, 1, 5),
+    ("az", 0, 0, 1), ("ay", 1, 0, 1), ("bz", 1, 5, 6), ("az", 0, 0, 5), ("hz0", 0, 2, "f"), ("ay", 1, 2, 1),
+    ("by", 0, 2, 0), ("xo", 0, 2), ("bz", 1, 3, 2), ("by", 0, 2, 2), ("bz", 1, 3, 6), ("az", 0, 1, 2),
+    ("az", 0, 1, 6), ("bz", 1, 4, 3), ("ay", 1, 1, "f"), ("az", 1, 1, 4), ("az", 1, 1, 0), ("xo", 1, 1),
+    ("az", 0, 0, 6), ("bz", 1, 5, 3), ("az", 0, 0, 2), ("ay", 1, 0, "f"), ("xo", 1, 0), ("az", 1, 0, 2),
+    ("bz", 1, 3, 3), ("az", 1, 0, 0), ("az", 1, 0, 3), ("az", 1, 0, 4), ("az", 0, 1, 3), ("az", 1, 0, 1),
+    ("bz", 1, 4, "f"), ("xo", 1, 4), ("by", 1, 4, 0), ("by", 1, 4, 1), ("by", 1, 4, 2), ("az", 1, 1, 5),
+    ("az", 1, 1, 1), ("ay", 1, 2, "f"), ("az", 1, 2, 1), ("az", 1, 2, 0), ("by", 0, 2, 1), ("xo", 1, 2),
+    ("az", 1, 2, 3), ("bz", 1, 5, "f"), ("by", 1, 5, 1), ("by", 1, 5, 0), ("az", 1, 2, 4), ("xo", 1, 5),
+    ("az", 0, 0, 3), ("by", 1, 5, 2), ("az", 1, 2, 2), ("az", 1, 0, 6), ("bz", 1, 3, "f"), ("xo", 1, 3),
+    ("by", 1, 3, 2), ("by", 1, 3, 1), ("by", 1, 3, 0), ("az", 1, 0, 5), ("az", 1, 1, 6), ("az", 0, 1, "f"),
+    ("az", 1, 1, 2), ("by", 1, 4, "f"), ("by", 0, 2, "f"), ("az", 1, 2, 5), ("az", 1, 2, 6),
+    ("az", 0, 0, "f"), ("ifin",), ("az", 1, 1, 3), ("az", 1, 0, "f"), ("by", 1, 5, "f"), ("by", 1, 3, "f"),
+    ("az", 1, 2, "f"), ("az", 1, 1, "f"),
 )
 
 
@@ -66,15 +63,29 @@
 
 
 STAGES = {"a": ("ay", "az"), "b": ("bz", "by"), "h": ("hz0", "hz1", "by")}
-RING = {"ay": (4, 8), "az": (8, 1), "bz": (8, 4), "hz0": (8, 2), "hz1": (8, 2), "by": (4, 1)}
+COUNT = {"ay": 8, "az": 1, "bz": 4, "hz0": 2, "hz1": 2, "by": 1}
 LAST = ("az", "by")
+PLANS = {
+    "yr": ((2, 1, ()), (1, 1, (0,)), (-1, -1, ())),
+    "yt": ((2, 2, ()), (1, 1, ()), (-1, -1, ())),
+    "zr": ((4, 1, ()), (3, 1, (0,)), (2, 1, (1,)), (1, 1, (2,)), (-3, -1, ()), (-2, -1, (4,)), (-1, -1, (5,))),
+    "zt": ((4, 2, ()), (3, 1, ()), (-3, -1, ()), (1, 1, ()), (-1, -1, ()), (2, 2, (0, 1)), (-2, -2, (2,))),
+}
+
+
+def plan_of(stage, way):
+    return PLANS[("y" if stage[1] == "y" else "z") + (way if stage in LAST else "r")]
+
+
+def ends_of(plan):
+    return [i for i, (owner, to, _) in enumerate(plan) if owner == to]
 
 
 def streams():
     for ph, cut in enumerate(STREAMS):
         first = 0
-        for s, (kind, width) in enumerate(cut):
-            yield ph, s, kind, first, width
+        for s, (kind, width, way) in enumerate(cut):
+            yield ph, s, kind, first, width, way
             first += width
 
 
@@ -84,8 +95,8 @@
     rest = list(scratch[16:])
     buffers = {}
     spans = {}
-    for ph, s, kind, first, width in streams():
-        spans[ph, s] = pl.ds(first, width), width
+    for ph, s, kind, first, width, way in streams():
+        spans[ph, s] = pl.ds(first, width), width, way
         for stage in STAGES[kind]:
             buffers[stage, ph, s], rest = rest[:4], rest[4:]
 
@@ -98,21 +109,28 @@
     x_lo_peer = {"dp": d, "fsdp": (1 - x_lo) * 2 + core}
     x_hi_peer = {"dp": (1 - x_hi) * 32 + y * 8 + z, "fsdp": f}
 
-    def y_peer(step, across=0):
-        return {"dp": (x_hi + across) % 2 * 32 + ((y + 4 + step) % 4) * 8 + z, "fsdp": f}
-
-    def z_peer(step, across=0):
-        return {"dp": (x_hi + across) % 2 * 32 + y * 8 + (z + 8 + step) % 8, "fsdp": f}
+    y_at = {k: (y + 4 + turn * k) % 4 for k in range(-2, 3)}
+    z_at = {k: (z + 8 + turn * k) % 8 for k in range(-4, 5)}
+    away = {ph: (mine + ph) % 2 for ph in (0, 1)}
+    sides = {None: x_hi, 0: (x_lo + 0) % 2, 1: (x_lo + 1) % 2, "x": 1 - x_hi}
+    y_dev = {(k, s): {"dp": x * 32 + y_at[k] * 8 + z, "fsdp": f} for k in (-2, -1, 1, 2) for s, x in sides.items()}
+    z_dev = {(k, s): {"dp": x * 32 + y * 8 + z_at[k], "fsdp": f} for k in (-2, -1, 1, 2) for s, x in sides.items()}
 
     barrier = pltpu.get_barrier_semaphore()
     partners = [other_core, x_lo_peer, x_hi_peer]
-    partners += [peer(step, side) for peer in (y_peer, z_peer) for step in (1, -1) for side in (0, 1)]
-    for p in partners:
-        pl.semaphore_signal(barrier, inc=1, device_id=p, device_id_type=MESH)
+    far = {"y": 1, "z": 1}
+    for _, _, kind, _, _, way in streams():
+        last = STAGES[kind][-1]
+        far[last[1]] = max(far[last[1]], *(to for _, to, _ in plan_of(last, way)))
+    for dev, reach in ((y_dev, far["y"]), (z_dev, far["z"])):
+        steps = [k for k in (1, -1, 2, -2) if abs(k) <= reach and (dev is z_dev or k != -2)]
+        partners += [dev[k, side] for k in steps for side in (None, "x")]
     load_x = pltpu.make_async_copy(x_hbm, x_in, ld_sem.at[0])
     load_x.start()
     load_c = pltpu.make_async_copy(c_hbm, cot, ld_sem.at[1])
     load_c.start()
+    for p in partners:
+        pl.semaphore_signal(barrier, inc=1, device_id=p, device_id_type=MESH)
     blocks = ((1 - x_lo) * 2 + (1 - core), (1 - x_lo) * 2 + core, x_lo * 2 + (1 - core), f)
     load_w = []
     for i, b in enumerate(blocks):
@@ -140,7 +158,7 @@
             pl.loop(0, n)(body)
 
     def grad_block(ph, s, block):
-        span, width = spans[ph, s]
+        span, width, _ = spans[ph, s]
         half = core if block == 0 else 1 - core
         tile = 256 if width % 256 == 0 else width
 
@@ -181,75 +199,75 @@
         return ph, to, z, slice(None), cols
 
     def ring(stage):
-        n, count = RING[stage]
-        return (n, count, y, y_peer) if stage[1] == "y" else (n, count, z, z_peer)
-
-    def slot_of(n, way, k):
-        return k if way > 0 else n // 2 + k - 1
-
-    def came(stage, ph, s, way, k):
-        n, _, _, peer = ring(stage)
+        return (y_at, y_dev) if stage[1] == "y" else (z_at, z_dev)
+
+    def came(stage, ph, s, m):
         s_buf, r_buf, ss, rs = buffers[stage, ph, s]
-        m = slot_of(n, way, k)
-        copy_to(s_buf.at[m], r_buf.at[m], ss.at[m], rs.at[m], peer(way * turn)).wait_recv()
+        copy_to(s_buf.at[0], r_buf.at[m], ss.at[0], rs.at[m], x_hi_peer).wait_recv()
         return r_buf.at[m]
 
-    def hop(stage, ph, s, way, k):
-        n, count, place, peer = ring(stage)
+    ready = set()
+
+    def message(stage, ph, s, m, only_encode=False):
+        places, devices = ring(stage)
         s_buf, r_buf, ss, rs = buffers[stage, ph, s]
-        to = (place + n + way * turn * (n // 2 - k)) % n
-        m = slot_of(n, way, k)
-        first = k == (0 if way > 0 else 1)
-        got = None if first else came(stage, ph, s, way, k - 1)
+        plan = plan_of(stage, spans[ph, s][2])
+        owner, to, joins = plan[m]
+        chunk = places[owner]
+        got = [came(stage, ph, s, i) for i in joins]
 
         def body(i):
-            part = g[view(stage, ph, s, to, i)]
-            if not first:
-                part = part + decode(got[i])
+            part = g[view(stage, ph, s, chunk, i)]
+            for other in got:
+                part = part + decode(other[i])
             s_buf[m, i] = encode(part)
 
-        pieces(count, body)
-        if stage in LAST and k == n // 2 - 1:
-            away = (mine + ph) % 2
-            to_slot = m + away * ((n - 1 if way > 0 else n) - m)
-            send(s_buf.at[m], r_buf.at[to_slot], ss.at[m], rs.at[to_slot], peer(way * turn, away))
+        if (stage, ph, s, m) not in ready:
+            pieces(COUNT[stage], body)
+        if only_encode:
+            ready.add((stage, ph, s, m))
+            return
+        if stage in LAST and owner == to:
+            slot = m + away[ph] * (len(plan) + ends_of(plan).index(m) - m)
+            send(s_buf.at[m], r_buf.at[slot], ss.at[m], rs.at[slot], devices[to, ph])
         else:
-            send(s_buf.at[m], r_buf.at[m], ss.at[m], rs.at[m], peer(way * turn))
+            send(s_buf.at[m], r_buf.at[m], ss.at[m], rs.at[m], devices[to, None])
 
     def finish(stage, ph, s):
-        n, count, place, _ = ring(stage)
-        last = [came(stage, ph, s, way, n // 2 - 1) for way in (1, -1)]
+        place = ring(stage)[0][0]
+        plan = plan_of(stage, spans[ph, s][2])
+        last = [came(stage, ph, s, m) for m in ends_of(plan)]
 
         def body(i):
             own = view(stage, ph, s, place, i)
             g[own] = g[own] + decode(last[0][i]) + decode(last[1][i])
 
-        pieces(count, body)
+        pieces(COUNT[stage], body)
 
     def own_part(stage, ph, s):
-        n, _, place, _ = ring(stage)
+        place = ring(stage)[0][0]
         s_buf, r_buf, ss, rs = buffers[stage, ph, s]
-        copy = copy_to(s_buf.at[n - 1], r_buf.at[n + 1], ss.at[n - 1], rs.at[n + 1], x_hi_peer)
-        return view(stage, ph, s, place, 0), s_buf, copy
+        plan = plan_of(stage, spans[ph, s][2])
+        m, slot = len(plan), len(plan) + len(ends_of(plan))
+        copy = copy_to(s_buf.at[m], r_buf.at[slot], ss.at[m], rs.at[slot], x_hi_peer)
+        return view(stage, ph, s, place, 0), s_buf.at[m], copy
 
     def own_across(stage, ph, s):
         @pl.when(mine != ph)
         def _():
-            own, s_buf, copy = own_part(stage, ph, s)
-            s_buf[RING[stage][0] - 1, 0] = encode(g[own])
+            own, buffer, copy = own_part(stage, ph, s)
+            buffer[0] = encode(g[own])
             copy.start()
 
     def last_finish(stage, ph, s):
-        n, _, place, _ = ring(stage)
-        s_buf, r_buf, ss, rs = buffers[stage, ph, s]
+        plan = plan_of(stage, spans[ph, s][2])
+        ends = ends_of(plan)
 
         @pl.when(mine == ph)
         def _():
-            total = g[view(stage, ph, s, place, 0)]
-            slots = (slot_of(n, 1, n // 2 - 1), slot_of(n, -1, n // 2 - 1), n - 1, n, n + 1)
-            for m in slots:
-                copy_to(s_buf.at[0], r_buf.at[m], ss.at[0], rs.at[m], x_hi_peer).wait_recv()
-                total = total + decode(r_buf[m, 0])
+            total = g[view(stage, ph, s, ring(stage)[0][0], 0)]
+            for m in ends + [len(plan) + i for i in range(len(ends) + 1)]:
+                total = total + decode(came(stage, ph, s, m)[0])
             grad_out[:, spans[ph, s][0]] = total * norm
 
     def to_buffer(buf, k):
@@ -263,7 +281,6 @@
     def send_features():
         flight["core"] = send(xt.at[0], xt.at[1], xt_ss.at[0], xt_rs.at[0], other_core)
         flight["chip"] = send(xt.at[0], xt.at[2], xt_ss.at[1], xt_rs.at[1], x_lo_peer)
-        load_c.wait()
 
     def pass_features():
         flight["chip"].wait_recv()
@@ -296,6 +313,14 @@
 
     load_x.wait()
     xt[0] = (x_in[...] * jnp.array(LIFT, BF16)).T
+    load_c.wait()
+    first = [at for at in ORDER if at[0] == "mg" and at[1] == at[3] == 0]
+    for at in first:
+        grad_block(*at[1:])
+    for stage, *at in ORDER:
+        if stage == "hz0" and at[0] == 0 and at[2] != "f":
+            if not plan_of(stage, "r")[at[2]][2]:
+                message(stage, *at, only_encode=True)
     pl.semaphore_wait(barrier, len(partners))
 
     waits = {(0, 1): "core", (1, 1): "pass"}
@@ -313,6 +338,8 @@
             input_grad_sum()
         elif what == "mg":
             ph, s, block = at
+            if ph == block == 0:
+                continue
             key = waits.get((ph, block))
             if key and key not in waited:
                 flight[key].wait_recv()
@@ -323,7 +350,7 @@
         elif at[2] == "f":
             (last_finish if what in LAST else finish)(what, *at[:2])
         else:
-            hop(what, at[0], at[1], 1 if at[2] == "m" else -1, at[3])
+            message(what, *at)
     for copy in sends:
         copy.wait_send()
     for ph, s, kind, *_ in streams():
@@ -337,10 +364,12 @@
     dma = pltpu.SemaphoreType.DMA
     nm = lambda *s: pltpu.VMEM(s, BF16)
     rings = []
-    for _, _, kind, _, width in streams():
+    for _, _, kind, _, width, way in streams():
         for stage in STAGES[kind]:
-            n, count = RING[stage]
-            sent, came = (n, n + 2) if stage in LAST else (n - 1, n - 1)
+            plan, count = plan_of(stage, way), COUNT[stage]
+            sent = came = len(plan)
+            if stage in LAST:
+                sent, came = sent + 1, came + len(ends_of(plan)) + 1
             rings += [nm(sent, count, 32, width), nm(came, count, 32, width), dma((sent,)), dma((came,))]
     any_ = pl.BlockSpec(memory_space=pl.ANY)
     vm = pl.BlockSpec(memory_space=pltpu.VMEM)

time: 70.5 us -> 69.7 us (0.989)
    pallas_call x1, Pallas kernels: 67.5 us -> 66.7 us  [reduce_all(): pl.pallas_call(lambda *refs: kernel(norm, *refs), out_shape=(jax.ShapeDty...]
where the time goes in v2:
time: 69.7 us; the launch traced here: 69.6 us
  Pallas kernels  69 us (99%)
    pallas_call x1, Pallas kernels, reduce_all(): pl.pallas_call(lambda *refs: kernel(norm, *refs), out_shape=(jax.ShapeDty...  66.7 us
    pallas_call x1, Pallas kernels, update(): pl.pallas_call(update_kernel, out_shape=(like(master), like(first), like(...  2.29 us

profile of v2, /device:TPU:2, one launch (start us, length us, event | category | flops | bytes accessed | tf_op | source)
XLA Modules:
  0.0 69.6 jit_solution(12169610992406243952)
XLA Ops:
  0.6 66.7 %reduce_all.1 = (f32[32,1792]{1,0:T(8,128)}, bf16[512,512]{1,0:T(8,128)(2,1)}) custom-call(bf16[512,512]{1,0:T(8,128)(2,1)} %refs_0_.1, bf16[512,1792]{1,0:T(8,128)(2,1)} %refs_1_.1, bf16[2048,1792]{1,0:T(8,128)(2,1)} %refs_2_.1), custom_call_target="tpu_custom_call" | custom-call | flops 7516192768 | bytes 12000000 | tf_op jit(solution)/shard_map/reduce_all/pallas_call | solution.py:376
  67.3 2.3 %update.1 = (f32[32,1792]{1,0:T(8,128)}, f32[32,1792]{1,0:T(8,128)}, f32[32,1792]{1,0:T(8,128)}, bf16[512,512]{1,0:T(8,128)(2,1)}) custom-call(f32[32,1792]{1,0:T(8,128)} %get-tuple-element.10.grad, f32[32,1792]{1,0:T(8,128)} %master.1, f32[32,1792]{1,0:T(8,128)} %first.1, f32[32,1792]{1,0:T(8,128)} %second.1, bf16[512,512]{1,0:T(8,128)(2,1)} %get-tuple-element.11.ig), custom_call_target="tpu_custom_call" | custom-call | tf_op jit(solution)/shard_map/update/pallas_call | solution.py:410

commit v3 on v2

--- a/solution.py
+++ b/solution.py
@@ -92,7 +92,9 @@
 def kernel(norm, x_hbm, c_hbm, w_hbm, grad_out, ig_out, *scratch):
     x_in, xt, cot, w, g, pc_s, pc_r, pp_s, pp_r = scratch[:9]
     ld_sem, xt_ss, xt_rs, pc_ss, pc_rs, pp_ss, pp_rs = scratch[9:16]
-    rest = list(scratch[16:])
+    rest = list(scratch[16:-2])
+    ig_buf, ig_sem = scratch[-2:]
+    write_ig = pltpu.make_async_copy(ig_buf, ig_out, ig_sem)
     buffers = {}
     spans = {}
     for ph, s, kind, first, width, way in streams():
@@ -307,9 +309,10 @@
 
         def body(rows):
             total = pp_s[1, rows, :] + pc_r[1, rows, :] + pp_r[0, rows, :]
-            ig_out[rows, :] = total.astype(BF16)
+            ig_buf[rows, :] = total.astype(BF16)
 
         rows_loop(body)
+        write_ig.start()
 
     load_x.wait()
     xt[0] = (x_in[...] * jnp.array(LIFT, BF16)).T
@@ -351,6 +354,7 @@
             (last_finish if what in LAST else finish)(what, *at[:2])
         else:
             message(what, *at)
+    write_ig.wait()
     for copy in sends:
         copy.wait_send()
     for ph, s, kind, *_ in streams():
@@ -380,7 +384,7 @@
             jax.ShapeDtypeStruct((TOK, FEAT), BF16),
         ),
         in_specs=[any_, any_, any_],
-        out_specs=(vm, vm),
+        out_specs=(vm, any_),
         scratch_shapes=[
             nm(TOK, FEAT), nm(4, FEAT, TOK), nm(TOK, COLS), nm(4, FEAT, COLS),
             pltpu.VMEM((2, 4, 8, 32, COLS), F32),
@@ -389,6 +393,7 @@
             dma((6,)), dma((3,)), dma((3,)),
             dma((2,)), dma((2,)), dma((1,)), dma((1,)),
             *rings,
+            nm(TOK, FEAT), dma,
         ],
         compiler_params=pltpu.CompilerParams(
             collective_id=1, has_side_effects=True, vmem_limit_bytes=60 * 2**20

time: 69.7 us -> 69.6 us (level)
  no operation moved by 1% of the time
where the time goes in v3:
time: 69.6 us; the launch traced here: 69.5 us
  Pallas kernels  68.8 us (99%)
    pallas_call x1, Pallas kernels, reduce_all(): pl.pallas_call(lambda *refs: kernel(norm, *refs), out_shape=(jax.ShapeDty...  66.5 us
    pallas_call x1, Pallas kernels, update(): pl.pallas_call(update_kernel, out_shape=(like(master), like(first), like(...  2.29 us

profile of v3, /device:TPU:2, one launch (start us, length us, event | category | flops | bytes accessed | tf_op | source)
XLA Modules:
  0.0 69.5 jit_solution(13411978772834203550)
XLA Ops:
  0.6 66.5 %reduce_all.1 = (f32[32,1792]{1,0:T(8,128)}, bf16[512,512]{1,0:T(8,128)(2,1)}) custom-call(bf16[512,512]{1,0:T(8,128)(2,1)} %refs_0_.1, bf16[512,1792]{1,0:T(8,128)(2,1)} %refs_1_.1, bf16[2048,1792]{1,0:T(8,128)(2,1)} %refs_2_.1), custom_call_target="tpu_custom_call" | custom-call | flops 7516192768 | bytes 12000000 | tf_op jit(solution)/shard_map/reduce_all/pallas_call | solution.py:380
  67.2 2.3 %update.1 = (f32[32,1792]{1,0:T(8,128)}, f32[32,1792]{1,0:T(8,128)}, f32[32,1792]{1,0:T(8,128)}, bf16[512,512]{1,0:T(8,128)(2,1)}) custom-call(f32[32,1792]{1,0:T(8,128)} %get-tuple-element.10.grad, f32[32,1792]{1,0:T(8,128)} %master.1, f32[32,1792]{1,0:T(8,128)} %first.1, f32[32,1792]{1,0:T(8,128)} %second.1, bf16[512,512]{1,0:T(8,128)(2,1)} %get-tuple-element.11.ig), custom_call_target="tpu_custom_call" | custom-call | tf_op jit(solution)/shard_map/update/pallas_call | solution.py:415
